TPU v7x, 32 devices: a whole 2x2x4 slice. The times are simulated.
32 devices in a mesh: gx: 2 (over y), gy: 16 (over z, x, core).
Axes of the slice: x: 2, y: 2, z: 4, core: 2. Of those that a mesh axis runs over, the one named last changes fastest.
Arguments:
- disp: bfloat16 [10, 160, 26, 3], P('gx', 'gy'), may hold values from -6 to 6
- disp_prev: bfloat16 [10, 160, 26, 3], P('gx', 'gy'), may hold values from -6 to 6
- tangent: bfloat16 [10, 160, 4992], P('gx', 'gy'), may hold values from -6 to 6
- tangent_prev: bfloat16 [10, 160, 4992], P('gx', 'gy'), may hold values from -6 to 6
- lame_lambda: bfloat16 [2, 32, 5], P('gx', 'gy'), may hold values from 0.29882812 to 3
- lame_mu: bfloat16 [2, 32, 5], P('gx', 'gy'), may hold values from 0.29882812 to 3
- node_mass: float32 [10, 160, 26], P('gx', 'gy'), may hold values from 0.5 to 2
- force: bfloat16 [10, 160, 26, 3], P('gx', 'gy'), may hold values from -48 to 48
- cell_block: int32 [2, 32, 5], P('gx', 'gy'), may hold values from 0 to 63
- direction_block: int32 [64], replicated, may hold values from 0 to 63
- port_id: int32 [10, 160, 26], P('gx', 'gy'), may hold values from 0 to 64, as said below
- port_mode: bfloat16 [10, 160, 26, 3], P('gx', 'gy'), may hold values from -0.059814453 to 0.059814453
Outputs:
- disp_next: bfloat16 [10, 160, 26, 3], P('gx', 'gy')
- tangent_next: bfloat16 [10, 160, 4992], P('gx', 'gy')
- port_amp: float32 [64, 64], P('gy', 'gx')
Inputs may be any that keep to these rules, and one draw needn't show every extreme that they name: `port_id`: 64 marks a node outside every output section; the output sections are the last 40 node layers along the second dimension, where every node belongs to some port; within each node line along the first dimension the port numbers never fall.
All inputs are finite; a program needn't handle non-finite values.
Results may differ from a plain program's by a relative error of at most 0.0016.
Values may be sent and summed in bfloat16 or wider, within the bound.
A program may use at most 192 MiB of HBM per device.

v0:
```python
import functools

import jax
import jax.numpy as jnp
import numpy as np
from jax import lax
from jax.experimental import pallas as pl
from jax.experimental.pallas import tpu as pltpu
from jax.sharding import PartitionSpec as P

PORTS = 64
PORT_DEPTH = 40
EZ = 5
NT = 64
NZN = 26
GLL_POINTS = np.array(
    [-1.0, -0.765055323929465, -0.285231516480645, 0.285231516480645, 0.765055323929465, 1.0]
)
GLL_WEIGHTS = np.array(
    [
        1.0 / 15.0,
        0.378474956297847,
        0.554858377035486,
        0.554858377035486,
        0.378474956297847,
        1.0 / 15.0,
    ]
)
STEP_SQUARED = 0.03
MESH = pl.DeviceIdType.MESH
F32 = jnp.float32
BF16 = jnp.bfloat16
COLS = 3 * NZN * NT
WIDE = COLS + 128
SPLITS = 2
PAIRS = ((0, 1), (2, 3), (5, 6), (7, 8), (4, 9))


def derivative_table():
    identity = np.eye(6)
    differences = GLL_POINTS[:, None] - GLL_POINTS[None, :] + identity
    barycentric = 1.0 / np.prod(differences, axis=1)
    matrix = barycentric[None, :] / barycentric[:, None] / differences
    matrix = matrix * (1.0 - identity)
    matrix = matrix - identity * matrix.sum(axis=1)[:, None]
    return matrix


def split_bf16(table):
    high = table.astype(jnp.bfloat16)
    low = (table - high.astype(np.float64)).astype(jnp.bfloat16)
    return [high, low]


def element_tables():
    d = derivative_table()
    eye = np.eye(6)
    ds = [
        np.kron(np.kron(d, eye), eye),
        np.kron(np.kron(eye, d), eye),
        np.kron(np.kron(eye, eye), d),
    ]
    w = np.kron(np.kron(GLL_WEIGHTS, GLL_WEIGHTS), GLL_WEIGHTS)[:, None]
    lap = sum(m.T @ (w * m) for m in ds)
    both = np.zeros((2, 216, 3, 216, 3))
    for c in range(3):
        for e in range(3):
            both[0, :, c, :, e] = ds[c].T @ (w * ds[e])
            both[1, :, c, :, e] = ds[e].T @ (w * ds[c]) + (lap if c == e else 0.0)
    both = both.reshape(2, 6, 6, 6, 3, 6, 6, 6, 3)
    both = both.transpose(0, 1, 3, 4, 2, 5, 7, 8, 6)
    pad = [(0, 0)] * 9
    pad[4] = (0, 2)
    pad[8] = (0, 2)
    both = np.pad(both, pad).reshape(2, 6, 144, 864)
    both = both.transpose(1, 0, 2, 3).reshape(6, 288, 864)
    return np.stack(split_bf16(both)[:SPLITS])


def layout_tables():
    expand = np.zeros((128, NZN, 3, NT))
    for k in range(NZN):
        for c in range(3):
            expand[c * 32 + k, k, c, :] = 1.0
    gather = np.zeros((2, 128, 18, 128))
    for ey in range(2):
        for ez in range(EZ):
            for kz in range(6):
                for c in range(3):
                    gather[ey, c * 32 + 5 * ez + kz, kz * 3 + c, ey * 5 + ez] = 1.0
    gather = gather.reshape(256, 18 * 128)
    return (
        expand.reshape(128, COLS).astype(jnp.bfloat16),
        gather.astype(jnp.bfloat16),
        np.ascontiguousarray(gather.T).astype(jnp.bfloat16),
    )


def lane_tile(t):
    return slice(t * 128, (t + 1) * 128)


def hi_lo(values):
    high = values.astype(BF16)
    return high, (values - high.astype(F32)).astype(BF16)


def dot(a, b):
    return jnp.dot(a, b, preferred_element_type=F32)


def kernel(
    nx, ny, nsrc_y,
    lame, cells, dirs, tan, tanp, prep, mass, pid, k_hbm, e_hbm, p_hbm, q_hbm,
    tan_out, disp_out, port_out,
    kv, ev, pv, qv, const_sem,
    txf, tpf, exf, wf, oh, uh, ul, ms, ps, dsc, z, o, fs, fpb,
    s1x, s1y, s1d, r1x, r1y, r1d, s2x, s2y, s2d, r2x, r2y, r2d,
    pbuf, prec, send_sem, recv_sem, psend, precv,
):
    gx = lax.axis_index("gx")
    gy = lax.axis_index("gy")
    consts = [
        pltpu.make_async_copy(a, b, const_sem.at[i])
        for i, (a, b) in enumerate(((e_hbm, ev), (p_hbm, pv), (k_hbm, kv), (q_hbm, qv)))
    ]
    for copy in consts:
        copy.start()

    x_lo, x_hi = gx > 0, gx < nx - 1
    y_lo, y_hi = gy > 0, gy < ny - 1
    first_src = ny - nsrc_y
    is_src = gy >= first_src
    n_all = nx * ny
    me = gx * ny + gy

    barrier = pltpu.get_barrier_semaphore()
    around = (
        (x_lo, -1, 0), (x_hi, 1, 0), (y_lo, 0, -1), (y_hi, 0, 1),
        (jnp.logical_and(x_lo, y_lo), -1, -1), (jnp.logical_and(x_hi, y_hi), 1, 1),
    )
    expected = jnp.int32(0)
    for there, dx, dy in around:
        @pl.when(there)
        def _(dx=dx, dy=dy):
            pl.semaphore_signal(barrier, inc=1, device_id=(gx + dx, gy + dy), device_id_type=MESH)
        expected = expected + there.astype(jnp.int32)

    def greet(s, carry):
        sx = s // nsrc_y
        sy = first_src + s % nsrc_y

        @pl.when(sx * ny + sy != me)
        def _():
            pl.semaphore_signal(barrier, inc=1, device_id=(sx, sy), device_id_type=MESH)
        return carry

    lax.fori_loop(0, nx * nsrc_y, greet, 0)
    expected = expected + is_src.astype(jnp.int32) * (n_all - 1)

    s1x[...] = jnp.zeros_like(s1x)
    s1y[...] = jnp.zeros_like(s1y)
    s1d[...] = jnp.zeros_like(s1d)
    s1x[0:10, 0:COLS] = tan[0]
    s1x[:, COLS:] = prep[0, 0]
    for x in range(5):
        s1y[x:x + 1, 0:COLS] = tan[x, 0:1, :]
        s1y[x:x + 1, COLS:] = prep[0, x, 0:1, :]
    row = jnp.concatenate([tan[0, 0:1, :], prep[0, 0, 0:1, :]], axis=1)
    for r in range(14):
        width = min(384, WIDE - r * 384)
        s1d[r:r + 1, 0:width] = row[:, r * 384:r * 384 + width]

    pl.semaphore_wait(barrier, expected)

    def remote(index, src, dst, dx, dy):
        return pltpu.make_async_remote_copy(
            src_ref=src, dst_ref=dst, send_sem=send_sem.at[index], recv_sem=recv_sem.at[index],
            device_id=(gx + dx, gy + dy), device_id_type=MESH,
        )

    first = (
        (remote(0, s1x, r1x, -1, 0), x_lo, x_hi, r1x),
        (remote(1, s1y, r1y, 0, -1), y_lo, y_hi, r1y),
        (remote(2, s1d, r1d, -1, -1), jnp.logical_and(x_lo, y_lo), jnp.logical_and(x_hi, y_hi), r1d),
    )
    second = (
        (remote(3, s2x, r2x, 1, 0), x_hi, x_lo, r2x),
        (remote(4, s2y, r2y, 0, 1), y_hi, y_lo, r2y),
        (remote(5, s2d, r2d, 1, 1), jnp.logical_and(x_hi, y_hi), jnp.logical_and(x_lo, y_lo), r2d),
    )

    def start(item):
        copy, sends, _, _ = item

        @pl.when(sends)
        def _():
            copy.start()

    def arrived(item):
        copy, _, receives, buffer = item

        @pl.when(receives)
        def _():
            copy.wait_recv()

        @pl.when(jnp.logical_not(receives))
        def _():
            buffer[...] = jnp.zeros_like(buffer)

    def sent(item):
        copy, sends, _, _ = item

        @pl.when(sends)
        def _():
            copy.wait_send()

    for item in first:
        start(item)

    lane = lax.broadcasted_iota(jnp.int32, (1, 128), 1)
    low_half = lane < 64

    def halves(a, b):
        return jnp.where(low_half, a, b)

    def prepare(x, carry):
        txf[x, 8:16, :] = jnp.zeros((8, WIDE), F32)
        tpf[x, 8:16, :] = jnp.zeros((8, COLS), F32)
        txf[x, 0:10, 0:COLS] = tan[x].astype(F32)
        txf[x, :, COLS:] = prep[0, x].astype(F32)
        tpf[x, 0:10, :] = tanp[x].astype(F32)
        ms[...] = jnp.ones_like(ms)
        ps[...] = jnp.full(ps.shape, PORTS, jnp.int32)
        ms[0:10, 0:NZN] = mass[x]
        ps[0:10, 0:NZN] = pid[x]
        rep_row = lax.broadcasted_iota(jnp.int32, (128, 128), 0)
        rep_col = lax.broadcasted_iota(jnp.int32, (128, 128), 1)
        rep = jnp.where((rep_col % 32 == rep_row) & (rep_row < NZN), 1.0, 0.0).astype(BF16)
        inv_hi, inv_lo = hi_lo(STEP_SQUARED / ms[...])
        exf[x, 0:16] = dot(inv_hi, rep).astype(BF16)
        exf[x, 16:32] = dot(inv_lo, rep).astype(BF16)
        exf[x, 32:48] = prep[3, x]
        ids = ps[...]
        rows = pl.ds(pl.multiple_of(x * 16, 16), 16)
        for pair in range(13):
            port = halves(ids[:, 2 * pair:2 * pair + 1], ids[:, 2 * pair + 1:2 * pair + 2])
            oh[pair, rows, :] = jnp.where(port == lane % 64, 1.0, 0.0).astype(BF16)
        return carry

    lax.fori_loop(0, 5, prepare, 0)

    consts[0].wait()
    lhs = exf[...].reshape(240, 128)

    def widen(n, carry):
        cols = pl.ds(pl.multiple_of(n * 384, 384), 384)
        w = dot(lhs, ev[:, cols]).reshape(5, 48, 384)
        wf[:, 0:16, cols] = w[:, 0:16] + w[:, 16:32]
        wf[:, 16:32, cols] = w[:, 32:48]
        return carry

    lax.fori_loop(0, COLS // 384, widen, 0)

    for item in first:
        arrived(item)
    for x in range(5):
        txf[x, 10:11, :] = r1y[x:x + 1, :].astype(F32)
    txf[5] = r1x[...].astype(F32)
    for r in range(14):
        width = min(384, WIDE - r * 384)
        txf[5, 10:11, r * 384:r * 384 + width] = r1d[r:r + 1, 0:width].astype(F32)

    consts[1].wait()
    near = jnp.concatenate([txf[x, 0:8, COLS:] for x in range(6)], axis=0)
    far = jnp.concatenate([txf[x, 5:13, COLS:] for x in range(6)], axis=0)
    gathered = dot(jnp.concatenate([near, far], axis=1).astype(BF16), pv[...])
    dsc[...] = gathered.reshape(6, 8, 18 * 128)

    def fill(x, carry):
        def tile(m, ey, ez):
            kc = 15 * ez + m
            return txf[x, 5 * ey:5 * ey + 8, lane_tile(kc // 2)]

        for mp in range(9):
            for i, (e1, e2) in enumerate(PAIRS):
                both = []
                for m in (2 * mp, 2 * mp + 1):
                    a, b = tile(m, e1 // 5, e1 % 5), tile(m, e2 // 5, e2 % 5)
                    a_half, b_half = (15 * (e1 % 5) + m) % 2, (15 * (e2 % 5) + m) % 2
                    if a_half == 0 and b_half == 1:
                        both.append(halves(a, b))
                    elif a_half == 1 and b_half == 0:
                        both.append(pltpu.roll(halves(b, a), 64, 1))
                    elif a_half == 0:
                        both.append(halves(a, pltpu.roll(b, 64, 1)))
                    else:
                        both.append(halves(pltpu.roll(a, 64, 1), b))
                z[x, 16 * mp:16 * mp + 16, lane_tile(i)] = jnp.concatenate(both, axis=0).astype(BF16)
            both = [dsc[x, :, lane_tile(2 * mp)], dsc[x, :, lane_tile(2 * mp + 1)]]
            z[x, 16 * mp:16 * mp + 16, lane_tile(5)] = jnp.concatenate(both, axis=0).astype(BF16)
        return carry

    lax.fori_loop(0, 6, fill, 0)
    consts[2].wait()

    def apply_far(n, carry):
        cols = pl.ds(pl.multiple_of(n * 256, 256), 256)
        rhs = z[:, :, cols].reshape(864, 256)
        o[5, :, cols] = sum(dot(kv[s, 5], rhs) for s in range(SPLITS))
        return carry

    def apply_near(n, carry):
        cols = pl.ds(pl.multiple_of(n * 256, 256), 256)
        rhs = z[:, :, cols].reshape(864, 256)
        for x in range(0, 5):
            o[x, :, cols] = sum(dot(kv[s, x], rhs) for s in range(SPLITS))
        return carry

    lam_rows = [halves(lame[a], lame[b]) for a, b in PAIRS]
    mu_rows = [halves(lame[10 + a], lame[10 + b]) for a, b in PAIRS]
    lam_point = sum(jnp.where(lane == e, lame[e], 0.0) for e in range(10))
    mu_point = sum(jnp.where(lane == e, lame[10 + e], 0.0) for e in range(10))
    sel_row = lax.broadcasted_iota(jnp.int32, (128, 128), 0)
    direction = dirs[...]
    choose = jnp.concatenate(
        [
            jnp.where(
                (sel_row == halves(a, b)) & (direction == halves(cells[a], cells[b])), 1.0, 0.0
            ).astype(BF16)
            for a, b in PAIRS
        ],
        axis=1,
    )

    def assemble(x):
        tile5 = o[x, 144:288, lane_tile(5)]
        point = lam_point * o[x, 0:144, lane_tile(5)] + mu_point * tile5
        point = jnp.concatenate([point[8 * m:8 * m + 8] for m in range(18)], axis=1)
        point_hi = point.astype(BF16).astype(F32)
        fpb[x] = jnp.concatenate([point_hi, point - point_hi], axis=0).astype(BF16)
        k_hi, k_lo = hi_lo(tile5)
        source = dot(k_hi, choose) + dot(k_lo, choose)
        force = [
            lam_rows[i] * o[x, 0:144, lane_tile(i)]
            + mu_rows[i] * o[x, 144:288, lane_tile(i)]
            + source[:, lane_tile(i)]
            for i in range(5)
        ]
        fs[x, 8:16, :] = jnp.zeros((8, WIDE), F32)
        for ey in range(2):
            for t in range(39):
                stay, move = ([], []), ([], [])
                for h in range(2):
                    kc = 2 * t + h
                    ez, m = kc // 15, kc % 15
                    for ez_at, m_at in ((ez, m), (ez - 1, m + 15)):
                        if 0 <= ez_at < EZ and m_at < 18:
                            e = ey * 5 + ez_at
                            i = next(n for n, p in enumerate(PAIRS) if e in p)
                            half = PAIRS[i].index(e)
                            piece = force[i][8 * m_at:8 * m_at + 8]
                            (stay if half == h else move)[half].append(piece)
                zero = jnp.zeros((8, 128), F32)
                total = halves(sum(stay[0], zero), sum(stay[1], zero))
                if move[0] or move[1]:
                    total = total + pltpu.roll(
                        halves(sum(move[0], zero), sum(move[1], zero)), 64, 1
                    )
                if ey == 0:
                    fs[x, 0:8, lane_tile(t)] = total
                else:
                    fs[x, 5:13, lane_tile(t)] = fs[x, 5:13, lane_tile(t)] + total

    def place_point(x, values):
        values = values[0:8] + values[8:16]
        fs[x, 0:8, COLS:] = values[:, 0:128]
        fs[x, 5:13, COLS:] = fs[x, 5:13, COLS:] + values[:, 128:256]

    lax.fori_loop(0, 3, apply_far, 0)
    assemble(5)
    consts[3].wait()
    place_point(5, dot(fpb[5], qv[...]))
    s2x[...] = fs[5].astype(BF16)
    s2d[...] = jnp.zeros_like(s2d)
    corner = fs[5, 10:11, :].astype(BF16)
    for r in range(14):
        width = min(384, WIDE - r * 384)
        s2d[r:r + 1, 0:width] = corner[:, r * 384:r * 384 + width]
    start(second[0])
    start(second[2])

    lax.fori_loop(0, 3, apply_near, 0)

    def assemble_near(x, carry):
        assemble(x)
        return carry

    lax.fori_loop(0, 5, assemble_near, 0)
    points = dot(fpb[0:5].reshape(80, 18 * 128), qv[...])
    s2y[...] = jnp.zeros_like(s2y)
    for x in range(5):
        place_point(x, points[16 * x:16 * x + 16])
        s2y[x:x + 1, :] = fs[x, 10:11, :].astype(BF16)
    start(second[1])

    for item in second:
        arrived(item)
    fs[0] = fs[0] + r2x[...].astype(F32)
    for x in range(5):
        fs[x, 0:1, :] = fs[x, 0:1, :] + r2y[x:x + 1, :].astype(F32)
    for r in range(14):
        width = min(384, WIDE - r * 384)
        cols = slice(r * 384, r * 384 + width)
        fs[0, 0:1, cols] = fs[0, 0:1, cols] + r2d[r:r + 1, 0:width].astype(F32)

    def finish(x, carry):
        scale = exf[x, 0:16].astype(F32) + exf[x, 16:32].astype(F32)
        moved = (
            2.0 * txf[x, :, COLS:]
            - prep[1, x].astype(F32)
            + scale * (prep[2, x].astype(F32) - fs[x, :, COLS:])
        )
        disp_out[x] = moved.astype(BF16)
        rows = pl.ds(pl.multiple_of(x * 16, 16), 16)
        for pair in range(13):
            parts = []
            for t in range(3 * pair, 3 * pair + 3):
                cols = lane_tile(t)
                full = 2.0 * txf[x, :, cols] - tpf[x, :, cols] - wf[x, 0:16, cols] * fs[x, :, cols]
                tan_out[x, :, cols] = full[0:10].astype(BF16)
                parts.append(full * wf[x, 16:32, cols])
            a, b, c = parts
            amount = halves(a + pltpu.roll(a, 64, 1), c + pltpu.roll(c, 64, 1)) + b
            high, low = hi_lo(amount)
            uh[pair, rows, :] = high
            ul[pair, rows, :] = low
        return carry

    lax.fori_loop(0, 5, finish, 0)

    per_row = PORTS // ny
    slot = gx * nsrc_y + (gy - first_src)

    def port_copy(target_x, target_y, slot_at):
        return pltpu.make_async_remote_copy(
            src_ref=pbuf.at[target_y], dst_ref=prec.at[slot_at],
            send_sem=psend.at[target_x * ny + target_y], recv_sem=precv.at[slot_at],
            device_id=(target_x, target_y), device_id_type=MESH,
        )

    @pl.when(is_src)
    def _():
        onehot = oh[...].reshape(1040, 128)
        dims = (((0,), (0,)), ((), ()))
        square = lax.dot_general(
            onehot, uh[...].reshape(1040, 128), dims, preferred_element_type=F32
        ) + lax.dot_general(onehot, ul[...].reshape(1040, 128), dims, preferred_element_type=F32)
        amp = square[0:64] + pltpu.roll(square[64:128], 64, 1)
        for g in range(ny):
            pbuf[g] = jnp.zeros((8, 128), F32)
            pbuf[g, 0:per_row, :] = amp[g * per_row:(g + 1) * per_row]

        def send(t, carry):
            @pl.when(t != me)
            def _():
                port_copy(t // ny, t % ny, slot).start()
            return carry

        lax.fori_loop(0, n_all, send, 0)
        prec[slot] = pbuf[gy]

    def collect(s, acc):
        @pl.when(jnp.logical_or(jnp.logical_not(is_src), s != slot))
        def _():
            port_copy(gx, gy, s).wait_recv()
        return acc + prec[s]

    acc = lax.fori_loop(0, nx * nsrc_y, collect, jnp.zeros((8, 128), F32))
    per_col = NT // nx
    mine = acc[0:per_row, 0:per_col]
    for h in range(1, nx):
        mine = jnp.where(gx == h, acc[0:per_row, h * per_col:(h + 1) * per_col], mine)
    port_out[...] = mine

    for item in first + second:
        sent(item)

    @pl.when(is_src)
    def _():
        def drain(t, carry):
            @pl.when(t != me)
            def _():
                port_copy(t // ny, t % ny, slot).wait_send()
            return carry

        lax.fori_loop(0, n_all, drain, 0)


def per_device(
    nx, ny,
    disp, disp_prev, tangent, tangent_prev, lame_lambda, lame_mu, node_mass, force,
    cell_block, direction_block, port_id, port_mode,
):
    rows = disp.shape[1]
    nsrc_y = -(-PORT_DEPTH // rows)
    lame = jnp.concatenate([lame_lambda.reshape(-1), lame_mu.reshape(-1)]).astype(F32)
    dirs = jnp.concatenate([direction_block, direction_block])[None]
    stacked = jnp.stack([disp, disp_prev, force, port_mode]).transpose(0, 1, 2, 4, 3)
    stacked = jnp.pad(stacked, ((0, 0), (0, 0), (0, 16 - rows), (0, 1), (0, 32 - NZN)))
    prep = stacked.reshape(4, 5, 16, 128)
    expand, gather, scatter = layout_tables()
    tables = element_tables()
    nsrc = nx * nsrc_y
    vmem = pl.BlockSpec(memory_space=pltpu.VMEM)
    smem = pl.BlockSpec(memory_space=pltpu.SMEM)
    hbm = pl.BlockSpec(memory_space=pl.ANY)
    big = pltpu.VMEM((16, WIDE), BF16)
    small = pltpu.VMEM((16, 384), BF16)
    tangent_next, moved, port_amp = pl.pallas_call(
        functools.partial(kernel, nx, ny, nsrc_y),
        out_shape=(
            jax.ShapeDtypeStruct(tangent.shape, BF16),
            jax.ShapeDtypeStruct((5, 16, 128), BF16),
            jax.ShapeDtypeStruct((PORTS // ny, NT // nx), F32),
        ),
        in_specs=[smem, smem] + [vmem] * 6 + [hbm] * 4,
        out_specs=(vmem, vmem, vmem),
        scratch_shapes=[
            pltpu.VMEM(tables.shape, BF16),
            pltpu.VMEM(expand.shape, BF16),
            pltpu.VMEM(gather.shape, BF16),
            pltpu.VMEM(scatter.shape, BF16),
            pltpu.SemaphoreType.DMA((4,)),
            pltpu.VMEM((6, 16, WIDE), F32),
            pltpu.VMEM((5, 16, COLS), F32),
            pltpu.VMEM((5, 48, 128), BF16),
            pltpu.VMEM((5, 32, COLS), F32),
            pltpu.VMEM((13, 80, 128), BF16),
            pltpu.VMEM((13, 80, 128), BF16),
            pltpu.VMEM((13, 80, 128), BF16),
            pltpu.VMEM((16, 128), F32),
            pltpu.VMEM((16, 128), jnp.int32),
            pltpu.VMEM((6, 8, 18 * 128), F32),
            pltpu.VMEM((6, 144, 768), BF16),
            pltpu.VMEM((6, 288, 768), F32),
            pltpu.VMEM((6, 16, WIDE), F32),
            pltpu.VMEM((6, 16, 18 * 128), BF16),
            big, big, small, big, big, small,
            big, big, small, big, big, small,
            pltpu.VMEM((ny, 8, 128), F32),
            pltpu.VMEM((nsrc, 8, 128), F32),
            pltpu.SemaphoreType.DMA((6,)),
            pltpu.SemaphoreType.DMA((6,)),
            pltpu.SemaphoreType.DMA((nx * ny,)),
            pltpu.SemaphoreType.DMA((nsrc,)),
        ],
        compiler_params=pltpu.CompilerParams(
            collective_id=0, has_side_effects=True, vmem_limit_bytes=56 * 1024 * 1024
        ),
    )(
        lame, cell_block.reshape(-1), dirs, tangent, tangent_prev, prep, node_mass, port_id,
        jnp.asarray(tables), jnp.asarray(expand), jnp.asarray(gather), jnp.asarray(scatter),
    )
    moved = moved.reshape(5, 16, 4, 32)[:, :rows, :3, :NZN].transpose(0, 1, 3, 2)
    return moved, tangent_next, port_amp


def solution(mesh):
    nx, ny = mesh.shape["gx"], mesh.shape["gy"]
    return jax.shard_map(
        functools.partial(per_device, nx, ny),
        mesh=mesh,
        in_specs=(
            P("gx", "gy", None, None),
            P("gx", "gy", None, None),
            P("gx", "gy", None),
            P("gx", "gy", None),
            P("gx", "gy", None),
            P("gx", "gy", None),
            P("gx", "gy", None),
            P("gx", "gy", None, None),
            P("gx", "gy", None),
            P(),
            P("gx", "gy", None),
            P("gx", "gy", None, None),
        ),
        out_specs=(P("gx", "gy", None, None), P("gx", "gy", None), P("gy", "gx")),
        check_vma=False,
    )
```

profile of v0, /device:TPU:0, one launch (start us, length us, event | category | flops | bytes accessed | tf_op | source)
XLA Modules:
  0.0 42.1 jit_solution(10717953218553335533)
XLA Ops:
  0.6 0.0 copy-start.2
  0.6 0.0 copy-start.3
  0.7 0.0 copy-start.4
  0.7 0.0 copy-start.1
  0.7 1.1 %maximum_bitcast_fusion = bf16[4,5,10,3,26]{4,3,2,1,0:T(4,128)(2,1)S(1)} fusion(bf16[1,5,10,26,3]{3,4,2,1,0:T(4,128)(2,1)} %bitcast.10, bf16[1,5,10,26,3]{3,4,2,1,0:T(4,128)(2,1)} %bitcast.11, bf16[1,5,10,26,3]{3,4,2,1,0:T(4,128)(2,1)} %bitcast.12, bf16[1,5,10,26,3]{3,4,2,1,0:T(4,128)(2,1)} %bitcast.13), kind=kLoop, calls=%fused_computation | loop fusion | flops 46800 | bytes 62400 | tf_op jit(solution)/shard_map/transpose | solution.py:509
  1.8 0.2 pad.4
  1.9 0.8 %reshape.24.prep = bf16[4,5,16,128]{3,2,1,0:T(8,128)(2,1)} reshape(bf16[4,5,16,4,32]{4,3,2,1,0:T(4,128)(2,1)S(1)} %pad.4) | data formatting | bytes 163840 | tf_op jit(solution)/shard_map/reshape | solution.py:511
  2.8 0.0 copy-done.2
  2.8 0.1 reshape.21
  2.9 0.0 copy-done.3
  2.9 0.1 reshape.22
  3.0 0.6 %maximum_convert_fusion.lame = f32[20]{0:T(128)} fusion(bf16[10]{0:T(256)(128)(2,1)S(1)} %reshape.22, bf16[10]{0:T(256)(128)(2,1)S(1)} %reshape.21), kind=kLoop, calls=%fused_computation.2 | loop fusion | flops 80 | bytes 120 | tf_op jit(solution)/shard_map/convert_element_type | solution.py:507
  3.6 0.0 copy-done.4
  3.6 0.6 %add_bitcast_fusion.dirs = s32[1,128]{1,0:T(1,128)} fusion(s32[64]{0:T(128)S(1)} %copy-done.4), kind=kLoop, calls=%fused_computation.3 | loop fusion | flops 128 | bytes 768 | tf_op jit(solution)/shard_map/broadcast_in_dim | solution.py:508
  4.2 0.0 copy-done.1
  4.2 0.6 %reshape.23.cells = s32[10]{0:T(128)} reshape(s32[1,2,5]{2,1,0:T(2,128)S(1)} %copy-done.1) | data formatting | bytes 80 | tf_op jit(solution)/shard_map/reshape | solution.py:562
  4.8 33.2 %shard_map.175 = (bf16[5,10,4992]{2,1,0:T(8,128)(2,1)}, bf16[5,16,128]{2,1,0:T(8,128)(2,1)}, f32[4,32]{1,0:T(4,128)}) custom-call(f32[20]{0:T(128)} %maximum_convert_fusion.lame, s32[10]{0:T(128)} %reshape.23.cells, s32[1,128]{1,0:T(1,128)} %add_bitcast_fusion.dirs, bf16[5,10,4992]{2,1,0:T(8,128)(2,1)} %tan.1, bf16[5,10,4992]{2,1,0:T(8,128)(2,1)} %tanp.1, ...), custom_call_target="tpu_custom_call" | custom-call | tf_op jit(solution)/shard_map/pallas_call | solution.py:520
  38.0 0.0 copy-start
  38.0 0.8 %reshape.25 = bf16[5,16,4,32]{3,2,1,0:T(4,128)(2,1)S(1)} reshape(bf16[5,16,128]{2,1,0:T(8,128)(2,1)} %get-tuple-element.6) | data formatting | bytes 40960 | tf_op jit(solution)/shard_map/reshape | solution.py:565
  38.8 0.6 %slice_bitcast_fusion = bf16[5,10,26,3]{2,3,1,0:T(4,128)(2,1)} fusion(bf16[5,16,4,32]{3,2,1,0:T(4,128)(2,1)S(1)} %reshape.25), kind=kLoop, calls=%fused_computation.1 | loop fusion | bytes 15600 | tf_op jit(solution)/shard_map/transpose | solution.py:565
  39.5 2.1 %copy.21 = bf16[5,10,4992]{2,1,0:T(8,128)(2,1)} copy(bf16[5,10,4992]{2,1,0:T(8,128)(2,1)} %get-tuple-element.13) | data formatting | bytes 998400
  41.5 0.0 copy-done
  41.5 0.6 %copy.22 = f32[4,32]{1,0:T(4,128)} copy(f32[4,32]{1,0:T(4,128)S(1)} %copy-done) | data formatting | bytes 1024
Async XLA Ops:
  0.6 2.2 %copy-start.2 = (bf16[1,2,5]{2,1,0:T(2,128)(2,1)S(1)}, bf16[1,2,5]{2,1,0:T(2,128)(2,1)}, u32[]{:S(2)}) copy-start(bf16[1,2,5]{2,1,0:T(2,128)(2,1)} %param.20) | copy-start | bytes 64
  0.6 2.2 %copy-start.3 = (bf16[1,2,5]{2,1,0:T(2,128)(2,1)S(1)}, bf16[1,2,5]{2,1,0:T(2,128)(2,1)}, u32[]{:S(2)}) copy-start(bf16[1,2,5]{2,1,0:T(2,128)(2,1)} %param.21) | copy-start | bytes 64
  0.7 2.9 %copy-start.4 = (s32[64]{0:T(128)S(1)}, s32[64]{0:T(128)}, u32[]{:S(2)}) copy-start(s32[64]{0:T(128)} %param.25) | copy-start | bytes 772
  0.7 3.5 %copy-start.1 = (s32[1,2,5]{2,1,0:T(2,128)S(1)}, s32[1,2,5]{2,1,0:T(2,128)}, u32[]{:S(2)}) copy-start(s32[1,2,5]{2,1,0:T(2,128)} %param.24) | copy-start | bytes 124
  38.0 3.6 %copy-start = (f32[4,32]{1,0:T(4,128)S(1)}, f32[4,32]{1,0:T(4,128)}, u32[]{:S(2)}) copy-start(f32[4,32]{1,0:T(4,128)} %get-tuple-element.14) | copy-start | bytes 1540
where the time goes:
time: 42.4 us; the launch traced here: 42.1 us
  Pallas kernels  33.2 us (78%)
  local copies, waits for them, and re-layouts  5.89 us (14%)
  other arithmetic  2.34 us (6%)
  between operations  0.71 us (2%)
    pallas_call x1, Pallas kernels, per_device(): pl.pallas_call(functools.partial(kernel, nx, ny, nsrc_y), out_shape=(jax....  33.2 us
    unnamed x12, local copies, waits for them, and re-layouts  2.67 us
    transpose x1, other arithmetic, per_device(): jnp.stack([disp, disp_prev, force, port_mode]).transpose(0, 1, 2, 4, 3)  1.1 us

commit v1 on v0

--- a/solution.py
+++ b/solution.py
@@ -96,6 +96,15 @@
     )
 
 
+X_PACK = (
+    (np.s_[0:10, 0:3200], np.s_[0:10, 0:3200]),
+    (np.s_[10:16, 0:1920], np.s_[0:6, 3200:5120]),
+    (np.s_[10:14, 1920:3200], np.s_[6:10, 3200:4480]),
+    (np.s_[14:16, 1920:2560], np.s_[6:8, 4480:5120]),
+    (np.s_[14:16, 2560:3200], np.s_[8:10, 4480:5120]),
+)
+
+
 def lane_tile(t):
     return slice(t * 128, (t + 1) * 128)
 
@@ -111,11 +120,11 @@
 
 def kernel(
     nx, ny, nsrc_y,
-    lame, cells, dirs, tan, tanp, prep, mass, pid, k_hbm, e_hbm, p_hbm, q_hbm,
+    lam_ref, mu_ref, cell_ref, dir_ref, tan, tanp, prep, mass, pid, k_hbm, e_hbm, p_hbm, q_hbm,
     tan_out, disp_out, port_out,
     kv, ev, pv, qv, const_sem,
     txf, tpf, exf, wf, oh, uh, ul, ms, ps, dsc, z, o, fs, fpb,
-    s1x, s1y, s1d, r1x, r1y, r1d, s2x, s2y, s2d, r2x, r2y, r2d,
+    s1x, s1y, s1d, r1x, r1y, r1d, s2x, s2y, s2d, s2p, r2x, r2y, r2d, r2p,
     pbuf, prec, send_sem, recv_sem, psend, precv,
 ):
     gx = lax.axis_index("gx")
@@ -158,11 +167,11 @@
     lax.fori_loop(0, nx * nsrc_y, greet, 0)
     expected = expected + is_src.astype(jnp.int32) * (n_all - 1)
 
-    s1x[...] = jnp.zeros_like(s1x)
     s1y[...] = jnp.zeros_like(s1y)
     s1d[...] = jnp.zeros_like(s1d)
-    s1x[0:10, 0:COLS] = tan[0]
-    s1x[:, COLS:] = prep[0, 0]
+    layer = jnp.concatenate([tan[0], prep[0, 0, 0:10, :]], axis=1)
+    for to, at in X_PACK:
+        s1x[to] = layer[at]
     for x in range(5):
         s1y[x:x + 1, 0:COLS] = tan[x, 0:1, :]
         s1y[x:x + 1, COLS:] = prep[0, x, 0:1, :]
@@ -186,8 +195,10 @@
     )
     second = (
         (remote(3, s2x, r2x, 1, 0), x_hi, x_lo, r2x),
-        (remote(4, s2y, r2y, 0, 1), y_hi, y_lo, r2y),
-        (remote(5, s2d, r2d, 1, 1), jnp.logical_and(x_hi, y_hi), jnp.logical_and(x_lo, y_lo), r2d),
+        (remote(4, s2d, r2d, 1, 1), jnp.logical_and(x_hi, y_hi), jnp.logical_and(x_lo, y_lo), r2d),
+        (remote(5, s2p, r2p, 0, 1), y_hi, y_lo, r2p),
+    ) + tuple(
+        (remote(6 + x, s2y.at[x], r2y.at[x], 0, 1), y_hi, y_lo, r2y.at[x]) for x in range(5)
     )
 
     def start(item):
@@ -262,20 +273,18 @@
 
     lax.fori_loop(0, COLS // 384, widen, 0)
 
-    for item in first:
-        arrived(item)
+    def gather_points(layers):
+        near = jnp.concatenate([txf[x, 0:8, COLS:] for x in layers], axis=0)
+        far = jnp.concatenate([txf[x, 5:13, COLS:] for x in layers], axis=0)
+        gathered = dot(jnp.concatenate([near, far], axis=1).astype(BF16), pv[...])
+        for n, x in enumerate(layers):
+            dsc[x] = gathered[8 * n:8 * n + 8]
+
+    arrived(first[1])
     for x in range(5):
         txf[x, 10:11, :] = r1y[x:x + 1, :].astype(F32)
-    txf[5] = r1x[...].astype(F32)
-    for r in range(14):
-        width = min(384, WIDE - r * 384)
-        txf[5, 10:11, r * 384:r * 384 + width] = r1d[r:r + 1, 0:width].astype(F32)
-
     consts[1].wait()
-    near = jnp.concatenate([txf[x, 0:8, COLS:] for x in range(6)], axis=0)
-    far = jnp.concatenate([txf[x, 5:13, COLS:] for x in range(6)], axis=0)
-    gathered = dot(jnp.concatenate([near, far], axis=1).astype(BF16), pv[...])
-    dsc[...] = gathered.reshape(6, 8, 18 * 128)
+    gather_points(range(5))
 
     def fill(x, carry):
         def tile(m, ey, ez):
@@ -301,28 +310,35 @@
             z[x, 16 * mp:16 * mp + 16, lane_tile(5)] = jnp.concatenate(both, axis=0).astype(BF16)
         return carry
 
-    lax.fori_loop(0, 6, fill, 0)
+    lax.fori_loop(0, 5, fill, 0)
+    arrived(first[0])
+    arrived(first[2])
+    txf[5, 8:16, :] = jnp.zeros((8, WIDE), F32)
+    for to, at in X_PACK:
+        txf[(5,) + at] = r1x[to].astype(F32)
+    for r in range(14):
+        width = min(384, WIDE - r * 384)
+        txf[5, 10:11, r * 384:r * 384 + width] = r1d[r:r + 1, 0:width].astype(F32)
+    gather_points([5])
+    fill(5, 0)
     consts[2].wait()
 
-    def apply_far(n, carry):
-        cols = pl.ds(pl.multiple_of(n * 256, 256), 256)
-        rhs = z[:, :, cols].reshape(864, 256)
-        o[5, :, cols] = sum(dot(kv[s, 5], rhs) for s in range(SPLITS))
-        return carry
-
-    def apply_near(n, carry):
-        cols = pl.ds(pl.multiple_of(n * 256, 256), 256)
-        rhs = z[:, :, cols].reshape(864, 256)
-        for x in range(0, 5):
-            o[x, :, cols] = sum(dot(kv[s, x], rhs) for s in range(SPLITS))
-        return carry
-
-    lam_rows = [halves(lame[a], lame[b]) for a, b in PAIRS]
-    mu_rows = [halves(lame[10 + a], lame[10 + b]) for a, b in PAIRS]
-    lam_point = sum(jnp.where(lane == e, lame[e], 0.0) for e in range(10))
-    mu_point = sum(jnp.where(lane == e, lame[10 + e], 0.0) for e in range(10))
+    def apply(x):
+        rhs = z[...].reshape(864, 768)
+        o[x] = sum(dot(kv[s, x], rhs) for s in range(SPLITS))
+
+    def per_element(values):
+        return [values[e // 5:e // 5 + 1, e % 5:e % 5 + 1] for e in range(10)]
+
+    lams = per_element(lam_ref[0].astype(F32))
+    mus = per_element(mu_ref[0].astype(F32))
+    cells = per_element(cell_ref[0])
+    lam_rows = [halves(lams[a], lams[b]) for a, b in PAIRS]
+    mu_rows = [halves(mus[a], mus[b]) for a, b in PAIRS]
+    lam_point = sum(jnp.where(lane == e, lams[e], 0.0) for e in range(10))
+    mu_point = sum(jnp.where(lane == e, mus[e], 0.0) for e in range(10))
     sel_row = lax.broadcasted_iota(jnp.int32, (128, 128), 0)
-    direction = dirs[...]
+    direction = jnp.concatenate([dir_ref[...], dir_ref[...]], axis=1)
     choose = jnp.concatenate(
         [
             jnp.where(
@@ -377,51 +393,42 @@
         fs[x, 0:8, COLS:] = values[:, 0:128]
         fs[x, 5:13, COLS:] = fs[x, 5:13, COLS:] + values[:, 128:256]
 
-    lax.fori_loop(0, 3, apply_far, 0)
+    def pack_row(buffer, values):
+        for r in range(-(-values.shape[1] // 384)):
+            width = min(384, values.shape[1] - r * 384)
+            buffer[r:r + 1, 0:width] = values[:, r * 384:r * 384 + width].astype(BF16)
+
+    s2d[...] = jnp.zeros_like(s2d)
+    s2y[...] = jnp.zeros_like(s2y)
+    s2p[...] = jnp.zeros_like(s2p)
+    apply(5)
+    consts[3].wait()
     assemble(5)
-    consts[3].wait()
+    apply(0)
     place_point(5, dot(fpb[5], qv[...]))
     s2x[...] = fs[5].astype(BF16)
-    s2d[...] = jnp.zeros_like(s2d)
-    corner = fs[5, 10:11, :].astype(BF16)
-    for r in range(14):
-        width = min(384, WIDE - r * 384)
-        s2d[r:r + 1, 0:width] = corner[:, r * 384:r * 384 + width]
+    pack_row(s2d, fs[5, 10:11, :])
     start(second[0])
-    start(second[2])
-
-    lax.fori_loop(0, 3, apply_near, 0)
-
-    def assemble_near(x, carry):
+    start(second[1])
+    for x in range(5):
+        if x < 4:
+            apply(x + 1)
         assemble(x)
-        return carry
-
-    lax.fori_loop(0, 5, assemble_near, 0)
+        pack_row(s2y.at[x], fs[x, 10:11, 0:COLS])
+        start(second[3 + x])
     points = dot(fpb[0:5].reshape(80, 18 * 128), qv[...])
-    s2y[...] = jnp.zeros_like(s2y)
     for x in range(5):
         place_point(x, points[16 * x:16 * x + 16])
-        s2y[x:x + 1, :] = fs[x, 10:11, :].astype(BF16)
-    start(second[1])
-
-    for item in second:
-        arrived(item)
-    fs[0] = fs[0] + r2x[...].astype(F32)
-    for x in range(5):
-        fs[x, 0:1, :] = fs[x, 0:1, :] + r2y[x:x + 1, :].astype(F32)
-    for r in range(14):
-        width = min(384, WIDE - r * 384)
-        cols = slice(r * 384, r * 384 + width)
-        fs[0, 0:1, cols] = fs[0, 0:1, cols] + r2d[r:r + 1, 0:width].astype(F32)
+        s2p[x:x + 1, :] = fs[x, 10:11, COLS:].astype(BF16)
+    start(second[2])
+
+    def add_row(x, buffer, width):
+        for r in range(-(-width // 384)):
+            size = min(384, width - r * 384)
+            cols = slice(r * 384, r * 384 + size)
+            fs[x, 0:1, cols] = fs[x, 0:1, cols] + buffer[r:r + 1, 0:size].astype(F32)
 
     def finish(x, carry):
-        scale = exf[x, 0:16].astype(F32) + exf[x, 16:32].astype(F32)
-        moved = (
-            2.0 * txf[x, :, COLS:]
-            - prep[1, x].astype(F32)
-            + scale * (prep[2, x].astype(F32) - fs[x, :, COLS:])
-        )
-        disp_out[x] = moved.astype(BF16)
         rows = pl.ds(pl.multiple_of(x * 16, 16), 16)
         for pair in range(13):
             parts = []
@@ -437,7 +444,31 @@
             ul[pair, rows, :] = low
         return carry
 
-    lax.fori_loop(0, 5, finish, 0)
+    def finish_points(x, carry):
+        fs[x, 0:1, COLS:] = fs[x, 0:1, COLS:] + r2p[x:x + 1, :].astype(F32)
+        scale = exf[x, 0:16].astype(F32) + exf[x, 16:32].astype(F32)
+        moved = (
+            2.0 * txf[x, :, COLS:]
+            - prep[1, x].astype(F32)
+            + scale * (prep[2, x].astype(F32) - fs[x, :, COLS:])
+        )
+        disp_out[x] = moved.astype(BF16)
+        return carry
+
+    for x in (1, 2, 3):
+        arrived(second[3 + x])
+        add_row(x, r2y.at[x], COLS)
+    lax.fori_loop(1, 4, finish, 0)
+    arrived(second[0])
+    arrived(second[1])
+    arrived(second[3])
+    fs[0] = fs[0] + r2x[...].astype(F32)
+    add_row(0, r2y.at[0], COLS)
+    add_row(0, r2d, WIDE)
+    finish(0, 0)
+    arrived(second[7])
+    add_row(4, r2y.at[4], COLS)
+    finish(4, 0)
 
     per_row = PORTS // ny
     slot = gx * nsrc_y + (gy - first_src)
@@ -470,6 +501,10 @@
         lax.fori_loop(0, n_all, send, 0)
         prec[slot] = pbuf[gy]
 
+    arrived(second[2])
+    for x in range(5):
+        finish_points(x, 0)
+
     def collect(s, acc):
         @pl.when(jnp.logical_or(jnp.logical_not(is_src), s != slot))
         def _():
@@ -497,6 +532,15 @@
         lax.fori_loop(0, n_all, drain, 0)
 
 
+def settle(tan, port, tan_out, port_out, sem):
+    copies = [pltpu.make_async_copy(tan.at[x], tan_out.at[x], sem.at[x]) for x in range(5)]
+    copies.append(pltpu.make_async_copy(port, port_out, sem.at[5]))
+    for copy in copies:
+        copy.start()
+    for copy in copies:
+        copy.wait()
+
+
 def per_device(
     nx, ny,
     disp, disp_prev, tangent, tangent_prev, lame_lambda, lame_mu, node_mass, force,
@@ -504,8 +548,6 @@
 ):
     rows = disp.shape[1]
     nsrc_y = -(-PORT_DEPTH // rows)
-    lame = jnp.concatenate([lame_lambda.reshape(-1), lame_mu.reshape(-1)]).astype(F32)
-    dirs = jnp.concatenate([direction_block, direction_block])[None]
     stacked = jnp.stack([disp, disp_prev, force, port_mode]).transpose(0, 1, 2, 4, 3)
     stacked = jnp.pad(stacked, ((0, 0), (0, 0), (0, 16 - rows), (0, 1), (0, 32 - NZN)))
     prep = stacked.reshape(4, 5, 16, 128)
@@ -513,10 +555,12 @@
     tables = element_tables()
     nsrc = nx * nsrc_y
     vmem = pl.BlockSpec(memory_space=pltpu.VMEM)
-    smem = pl.BlockSpec(memory_space=pltpu.SMEM)
     hbm = pl.BlockSpec(memory_space=pl.ANY)
     big = pltpu.VMEM((16, WIDE), BF16)
     small = pltpu.VMEM((16, 384), BF16)
+    packed = pltpu.VMEM((16, 3200), BF16)
+    rows5 = pltpu.VMEM((5, 16, 384), BF16)
+    point = pltpu.VMEM((16, 128), BF16)
     tangent_next, moved, port_amp = pl.pallas_call(
         functools.partial(kernel, nx, ny, nsrc_y),
         out_shape=(
@@ -524,7 +568,7 @@
             jax.ShapeDtypeStruct((5, 16, 128), BF16),
             jax.ShapeDtypeStruct((PORTS // ny, NT // nx), F32),
         ),
-        in_specs=[smem, smem] + [vmem] * 6 + [hbm] * 4,
+        in_specs=[vmem] * 9 + [hbm] * 4,
         out_specs=(vmem, vmem, vmem),
         scratch_shapes=[
             pltpu.VMEM(tables.shape, BF16),
@@ -546,12 +590,12 @@
             pltpu.VMEM((6, 288, 768), F32),
             pltpu.VMEM((6, 16, WIDE), F32),
             pltpu.VMEM((6, 16, 18 * 128), BF16),
-            big, big, small, big, big, small,
-            big, big, small, big, big, small,
+            packed, big, small, packed, big, small,
+            big, rows5, small, point, big, rows5, small, point,
             pltpu.VMEM((ny, 8, 128), F32),
             pltpu.VMEM((nsrc, 8, 128), F32),
-            pltpu.SemaphoreType.DMA((6,)),
-            pltpu.SemaphoreType.DMA((6,)),
+            pltpu.SemaphoreType.DMA((11,)),
+            pltpu.SemaphoreType.DMA((11,)),
             pltpu.SemaphoreType.DMA((nx * ny,)),
             pltpu.SemaphoreType.DMA((nsrc,)),
         ],
@@ -559,9 +603,19 @@
             collective_id=0, has_side_effects=True, vmem_limit_bytes=56 * 1024 * 1024
         ),
     )(
-        lame, cell_block.reshape(-1), dirs, tangent, tangent_prev, prep, node_mass, port_id,
+        lame_lambda, lame_mu, cell_block, direction_block[None], tangent, tangent_prev, prep, node_mass, port_id,
         jnp.asarray(tables), jnp.asarray(expand), jnp.asarray(gather), jnp.asarray(scatter),
     )
+    tangent_next, port_amp = pl.pallas_call(
+        settle,
+        out_shape=(
+            jax.ShapeDtypeStruct(tangent_next.shape, BF16),
+            jax.ShapeDtypeStruct(port_amp.shape, F32),
+        ),
+        in_specs=[hbm, hbm],
+        out_specs=(hbm, hbm),
+        scratch_shapes=[pltpu.SemaphoreType.DMA((6,))],
+    )(tangent_next, port_amp)
     moved = moved.reshape(5, 16, 4, 32)[:, :rows, :3, :NZN].transpose(0, 1, 3, 2)
     return moved, tangent_next, port_amp
 

time: 42.4 us -> 60.6 us (1.43)
  Pallas kernels: 33.2 us -> 56.1 us
  local copies, waits for them, and re-layouts: 5.89 us -> 2.46 us
  other arithmetic: 2.34 us -> 1.08 us
    pallas_call x0 -> x1, Pallas kernels: none -> 25.4 us  [per_device(): pl.pallas_call(settle, out_shape=(jax.ShapeDtypeStruct(tangent_next.shape...]
    unnamed x12 -> x0, local copies, waits for them, and re-layouts: 2.67 us -> none
    pallas_call x1, Pallas kernels: 33.2 us -> 30.7 us  [per_device(): pl.pallas_call(functools.partial(kernel, nx, ny, nsrc_y), out_shape=(jax....]
    reshape x3 -> x0, local copies, waits for them, and re-layouts: 0.76 us -> none  [the longest x1 0.59 us: per_device(): cell_block.reshape(-1)]
    broadcast_in_dim x1 -> x0, other arithmetic: 0.65 us -> none  [per_device(): dirs = jnp.concatenate([direction_block, direction_block])[None]]
where the time goes in v1:
time: 60.6 us; the launch traced here: 60.3 us
  Pallas kernels  56.1 us (93%)
  local copies, waits for them, and re-layouts  2.46 us (4%)
  other arithmetic  1.08 us (2%)
  between operations  0.67 us (1%)
    pallas_call x1, Pallas kernels, per_device(): pl.pallas_call(functools.partial(kernel, nx, ny, nsrc_y), out_shape=(jax....  30.7 us
    pallas_call x1, Pallas kernels, per_device(): pl.pallas_call(settle, out_shape=(jax.ShapeDtypeStruct(tangent_next.shape...  25.4 us

profile of v1, /device:TPU:0, one launch (start us, length us, event | category | flops | bytes accessed | tf_op | source)
XLA Modules:
  0.0 60.3 jit_solution(5301865158062222209)
XLA Ops:
  0.6 1.1 %maximum_bitcast_fusion = bf16[4,5,10,3,26]{4,3,2,1,0:T(4,128)(2,1)S(1)} fusion(bf16[1,5,10,26,3]{3,4,2,1,0:T(4,128)(2,1)} %bitcast.9, bf16[1,5,10,26,3]{3,4,2,1,0:T(4,128)(2,1)} %bitcast.10, bf16[1,5,10,26,3]{3,4,2,1,0:T(4,128)(2,1)} %bitcast.11, bf16[1,5,10,26,3]{3,4,2,1,0:T(4,128)(2,1)} %bitcast.12), kind=kLoop, calls=%fused_computation | loop fusion | flops 46800 | bytes 62400 | tf_op jit(solution)/shard_map/transpose | solution.py:551
  1.7 0.2 pad.4
  1.9 0.8 %reshape.12.prep = bf16[4,5,16,128]{3,2,1,0:T(8,128)(2,1)} reshape(bf16[4,5,16,4,32]{4,3,2,1,0:T(4,128)(2,1)S(1)} %pad.4) | data formatting | bytes 163840 | tf_op jit(solution)/shard_map/reshape | solution.py:553
  2.7 30.7 %shard_map.175 = (bf16[5,10,4992]{2,1,0:T(8,128)(2,1)}, bf16[5,16,128]{2,1,0:T(8,128)(2,1)}, f32[4,32]{1,0:T(4,128)}) custom-call(bf16[1,2,5]{2,1,0:T(2,128)(2,1)} %lam_ref.1, bf16[1,2,5]{2,1,0:T(2,128)(2,1)} %mu_ref.1, s32[1,2,5]{2,1,0:T(2,128)} %cell_ref.1, s32[1,64]{1,0:T(1,128)} %bitcast.13, bf16[5,10,4992]{2,1,0:T(8,128)(2,1)} %tan.1, ...), custom_call_target="tpu_custom_call" | custom-call | tf_op jit(solution)/shard_map/pallas_call | solution.py:564
  33.4 25.4 %shard_map.176 = (bf16[5,10,4992]{2,1,0:T(8,128)(2,1)}, f32[4,32]{1,0:T(4,128)}) custom-call(bf16[5,10,4992]{2,1,0:T(8,128)(2,1)} %get-tuple-element.9.tan, f32[4,32]{1,0:T(4,128)} %get-tuple-element.10.port), custom_call_target="tpu_custom_call" | custom-call | tf_op jit(solution)/shard_map/pallas_call | solution.py:609
  58.8 0.8 %reshape.13 = bf16[5,16,4,32]{3,2,1,0:T(4,128)(2,1)S(1)} reshape(bf16[5,16,128]{2,1,0:T(8,128)(2,1)} %get-tuple-element.8) | data formatting | bytes 40960 | tf_op jit(solution)/shard_map/reshape | solution.py:619
  59.7 0.6 %slice_bitcast_fusion = bf16[5,10,26,3]{2,3,1,0:T(4,128)(2,1)} fusion(bf16[5,16,4,32]{3,2,1,0:T(4,128)(2,1)S(1)} %reshape.13), kind=kLoop, calls=%fused_computation.1 | loop fusion | bytes 15600 | tf_op jit(solution)/shard_map/transpose | solution.py:619

commit v2 on v1

--- a/solution.py
+++ b/solution.py
@@ -69,11 +69,9 @@
             both[1, :, c, :, e] = ds[e].T @ (w * ds[c]) + (lap if c == e else 0.0)
     both = both.reshape(2, 6, 6, 6, 3, 6, 6, 6, 3)
     both = both.transpose(0, 1, 3, 4, 2, 5, 7, 8, 6)
-    pad = [(0, 0)] * 9
-    pad[4] = (0, 2)
-    pad[8] = (0, 2)
-    both = np.pad(both, pad).reshape(2, 6, 144, 864)
-    both = both.transpose(1, 0, 2, 3).reshape(6, 288, 864)
+    both = both.reshape(2, 6, 108, 6, 108)
+    both = np.pad(both, ((0, 0), (0, 0), (0, 4), (0, 0), (0, 4))).reshape(2, 6, 112, 672)
+    both = both.transpose(1, 0, 2, 3).reshape(6, 224, 672)
     return np.stack(split_bf16(both)[:SPLITS])
 
 
@@ -123,7 +121,7 @@
     lam_ref, mu_ref, cell_ref, dir_ref, tan, tanp, prep, mass, pid, k_hbm, e_hbm, p_hbm, q_hbm,
     tan_out, disp_out, port_out,
     kv, ev, pv, qv, const_sem,
-    txf, tpf, exf, wf, oh, uh, ul, ms, ps, dsc, z, o, fs, fpb,
+    txf, tpf, exf, wf, oh, oht, uu, ms, ps, dsc, z, o, zf, cf, fs, fpb,
     s1x, s1y, s1d, r1x, r1y, r1d, s2x, s2y, s2d, s2p, r2x, r2y, r2d, r2p,
     pbuf, prec, send_sem, recv_sem, psend, precv,
 ):
@@ -256,10 +254,14 @@
         rows = pl.ds(pl.multiple_of(x * 16, 16), 16)
         for pair in range(13):
             port = halves(ids[:, 2 * pair:2 * pair + 1], ids[:, 2 * pair + 1:2 * pair + 2])
-            oh[pair, rows, :] = jnp.where(port == lane % 64, 1.0, 0.0).astype(BF16)
+            oh[pair, rows, :] = jnp.where(port == lane % 64, 1.0, 0.0)
         return carry
 
     lax.fori_loop(0, 5, prepare, 0)
+
+    @pl.when(is_src)
+    def _():
+        oht[...] = oh[...].reshape(1040, 128).T.astype(BF16)
 
     consts[0].wait()
     lhs = exf[...].reshape(240, 128)
@@ -286,28 +288,29 @@
     consts[1].wait()
     gather_points(range(5))
 
+    zf[96:112, :] = jnp.zeros((16, 768), F32)
+
     def fill(x, carry):
         def tile(m, ey, ez):
             kc = 15 * ez + m
             return txf[x, 5 * ey:5 * ey + 8, lane_tile(kc // 2)]
 
-        for mp in range(9):
+        for m in range(18):
+            rows = slice(6 * m, 6 * m + 8)
             for i, (e1, e2) in enumerate(PAIRS):
-                both = []
-                for m in (2 * mp, 2 * mp + 1):
-                    a, b = tile(m, e1 // 5, e1 % 5), tile(m, e2 // 5, e2 % 5)
-                    a_half, b_half = (15 * (e1 % 5) + m) % 2, (15 * (e2 % 5) + m) % 2
-                    if a_half == 0 and b_half == 1:
-                        both.append(halves(a, b))
-                    elif a_half == 1 and b_half == 0:
-                        both.append(pltpu.roll(halves(b, a), 64, 1))
-                    elif a_half == 0:
-                        both.append(halves(a, pltpu.roll(b, 64, 1)))
-                    else:
-                        both.append(halves(pltpu.roll(a, 64, 1), b))
-                z[x, 16 * mp:16 * mp + 16, lane_tile(i)] = jnp.concatenate(both, axis=0).astype(BF16)
-            both = [dsc[x, :, lane_tile(2 * mp)], dsc[x, :, lane_tile(2 * mp + 1)]]
-            z[x, 16 * mp:16 * mp + 16, lane_tile(5)] = jnp.concatenate(both, axis=0).astype(BF16)
+                a, b = tile(m, e1 // 5, e1 % 5), tile(m, e2 // 5, e2 % 5)
+                a_half, b_half = (15 * (e1 % 5) + m) % 2, (15 * (e2 % 5) + m) % 2
+                if a_half == 0 and b_half == 1:
+                    both = halves(a, b)
+                elif a_half == 1 and b_half == 0:
+                    both = pltpu.roll(halves(b, a), 64, 1)
+                elif a_half == 0:
+                    both = halves(a, pltpu.roll(b, 64, 1))
+                else:
+                    both = halves(pltpu.roll(a, 64, 1), b)
+                zf[rows, lane_tile(i)] = both
+            zf[rows, lane_tile(5)] = dsc[x, :, lane_tile(m)]
+        z[x] = zf[...].astype(BF16)
         return carry
 
     lax.fori_loop(0, 5, fill, 0)
@@ -324,7 +327,7 @@
     consts[2].wait()
 
     def apply(x):
-        rhs = z[...].reshape(864, 768)
+        rhs = z[...].reshape(672, 768)
         o[x] = sum(dot(kv[s, x], rhs) for s in range(SPLITS))
 
     def per_element(values):
@@ -349,20 +352,26 @@
         axis=1,
     )
 
+    first_row = lax.broadcasted_iota(jnp.int32, (8, 128), 0) == 0
+
+    def merged(pieces):
+        low, high = [functools.reduce(jnp.add, p) if p else 0.0 for p in pieces]
+        return halves(low, high)
+
     def assemble(x):
-        tile5 = o[x, 144:288, lane_tile(5)]
-        point = lam_point * o[x, 0:144, lane_tile(5)] + mu_point * tile5
-        point = jnp.concatenate([point[8 * m:8 * m + 8] for m in range(18)], axis=1)
+        tile5 = o[x, 112:224, lane_tile(5)]
+        cf[0:112, lane_tile(5)] = lam_point * o[x, 0:112, lane_tile(5)] + mu_point * tile5
+        point = jnp.concatenate([cf[6 * m:6 * m + 8, lane_tile(5)] for m in range(18)], axis=1)
         point_hi = point.astype(BF16).astype(F32)
         fpb[x] = jnp.concatenate([point_hi, point - point_hi], axis=0).astype(BF16)
         k_hi, k_lo = hi_lo(tile5)
         source = dot(k_hi, choose) + dot(k_lo, choose)
-        force = [
-            lam_rows[i] * o[x, 0:144, lane_tile(i)]
-            + mu_rows[i] * o[x, 144:288, lane_tile(i)]
-            + source[:, lane_tile(i)]
-            for i in range(5)
-        ]
+        for i in range(5):
+            cf[0:112, lane_tile(i)] = (
+                lam_rows[i] * o[x, 0:112, lane_tile(i)]
+                + mu_rows[i] * o[x, 112:224, lane_tile(i)]
+                + source[:, lane_tile(i)]
+            )
         fs[x, 8:16, :] = jnp.zeros((8, WIDE), F32)
         for ey in range(2):
             for t in range(39):
@@ -375,23 +384,22 @@
                             e = ey * 5 + ez_at
                             i = next(n for n, p in enumerate(PAIRS) if e in p)
                             half = PAIRS[i].index(e)
-                            piece = force[i][8 * m_at:8 * m_at + 8]
+                            piece = cf[6 * m_at:6 * m_at + 8, lane_tile(i)]
                             (stay if half == h else move)[half].append(piece)
-                zero = jnp.zeros((8, 128), F32)
-                total = halves(sum(stay[0], zero), sum(stay[1], zero))
+                total = merged(stay)
                 if move[0] or move[1]:
-                    total = total + pltpu.roll(
-                        halves(sum(move[0], zero), sum(move[1], zero)), 64, 1
-                    )
+                    total = total + pltpu.roll(merged(move), 64, 1)
                 if ey == 0:
                     fs[x, 0:8, lane_tile(t)] = total
                 else:
-                    fs[x, 5:13, lane_tile(t)] = fs[x, 5:13, lane_tile(t)] + total
+                    shared = jnp.where(first_row, fs[x, 5:13, lane_tile(t)], 0.0)
+                    fs[x, 5:13, lane_tile(t)] = shared + total
 
     def place_point(x, values):
         values = values[0:8] + values[8:16]
         fs[x, 0:8, COLS:] = values[:, 0:128]
-        fs[x, 5:13, COLS:] = fs[x, 5:13, COLS:] + values[:, 128:256]
+        shared = jnp.where(first_row, fs[x, 5:13, COLS:], 0.0)
+        fs[x, 5:13, COLS:] = shared + values[:, 128:256]
 
     def pack_row(buffer, values):
         for r in range(-(-values.shape[1] // 384)):
@@ -440,8 +448,8 @@
             a, b, c = parts
             amount = halves(a + pltpu.roll(a, 64, 1), c + pltpu.roll(c, 64, 1)) + b
             high, low = hi_lo(amount)
-            uh[pair, rows, :] = high
-            ul[pair, rows, :] = low
+            uu[pair, rows, 0:128] = high
+            uu[pair, rows, 128:256] = low
         return carry
 
     def finish_points(x, carry):
@@ -482,11 +490,8 @@
 
     @pl.when(is_src)
     def _():
-        onehot = oh[...].reshape(1040, 128)
-        dims = (((0,), (0,)), ((), ()))
-        square = lax.dot_general(
-            onehot, uh[...].reshape(1040, 128), dims, preferred_element_type=F32
-        ) + lax.dot_general(onehot, ul[...].reshape(1040, 128), dims, preferred_element_type=F32)
+        square = dot(oht[...], uu[...].reshape(1040, 256))
+        square = square[:, 0:128] + square[:, 128:256]
         amp = square[0:64] + pltpu.roll(square[64:128], 64, 1)
         for g in range(ny):
             pbuf[g] = jnp.zeros((8, 128), F32)
@@ -532,13 +537,9 @@
         lax.fori_loop(0, n_all, drain, 0)
 
 
-def settle(tan, port, tan_out, port_out, sem):
-    copies = [pltpu.make_async_copy(tan.at[x], tan_out.at[x], sem.at[x]) for x in range(5)]
-    copies.append(pltpu.make_async_copy(port, port_out, sem.at[5]))
-    for copy in copies:
-        copy.start()
-    for copy in copies:
-        copy.wait()
+def settle(tan, port, tan_out, port_out):
+    tan_out[...] = tan[...]
+    port_out[...] = port[...]
 
 
 def per_device(
@@ -580,14 +581,16 @@
             pltpu.VMEM((5, 16, COLS), F32),
             pltpu.VMEM((5, 48, 128), BF16),
             pltpu.VMEM((5, 32, COLS), F32),
-            pltpu.VMEM((13, 80, 128), BF16),
-            pltpu.VMEM((13, 80, 128), BF16),
-            pltpu.VMEM((13, 80, 128), BF16),
+            pltpu.VMEM((13, 80, 128), F32),
+            pltpu.VMEM((128, 1040), BF16),
+            pltpu.VMEM((13, 80, 256), BF16),
             pltpu.VMEM((16, 128), F32),
             pltpu.VMEM((16, 128), jnp.int32),
             pltpu.VMEM((6, 8, 18 * 128), F32),
-            pltpu.VMEM((6, 144, 768), BF16),
-            pltpu.VMEM((6, 288, 768), F32),
+            pltpu.VMEM((6, 112, 768), BF16),
+            pltpu.VMEM((6, 224, 768), F32),
+            pltpu.VMEM((112, 768), F32),
+            pltpu.VMEM((112, 768), F32),
             pltpu.VMEM((6, 16, WIDE), F32),
             pltpu.VMEM((6, 16, 18 * 128), BF16),
             packed, big, small, packed, big, small,
@@ -612,9 +615,8 @@
             jax.ShapeDtypeStruct(tangent_next.shape, BF16),
             jax.ShapeDtypeStruct(port_amp.shape, F32),
         ),
-        in_specs=[hbm, hbm],
-        out_specs=(hbm, hbm),
-        scratch_shapes=[pltpu.SemaphoreType.DMA((6,))],
+        in_specs=[vmem, vmem],
+        out_specs=(vmem, vmem),
     )(tangent_next, port_amp)
     moved = moved.reshape(5, 16, 4, 32)[:, :rows, :3, :NZN].transpose(0, 1, 3, 2)
     return moved, tangent_next, port_amp

time: 60.6 us -> 34.5 us (0.57)
  Pallas kernels: 56.1 us -> 30 us
    pallas_call x1, Pallas kernels: 25.4 us -> 2.09 us  [per_device(): pl.pallas_call(settle, out_shape=(jax.ShapeDtypeStruct(tangent_next.shape...]
    pallas_call x1, Pallas kernels: 30.7 us -> 27.9 us  [per_device(): pl.pallas_call(functools.partial(kernel, nx, ny, nsrc_y), out_shape=(jax....]
where the time goes in v2:
time: 34.5 us; the launch traced here: 34.2 us
  Pallas kernels  30 us (87%)
  local copies, waits for them, and re-layouts  2.46 us (7%)
  other arithmetic  1.08 us (3%)
  between operations  0.66 us (2%)
    pallas_call x1, Pallas kernels, per_device(): pl.pallas_call(functools.partial(kernel, nx, ny, nsrc_y), out_shape=(jax....  27.9 us
    pallas_call x1, Pallas kernels, per_device(): pl.pallas_call(settle, out_shape=(jax.ShapeDtypeStruct(tangent_next.shape...  2.09 us
    transpose x1, other arithmetic, per_device(): jnp.stack([disp, disp_prev, force, port_mode]).transpose(0, 1, 2, 4, 3)  1.08 us
    reshape x1, local copies, waits for them, and re-layouts, per_device(): prep = stacked.reshape(4, 5, 16, 128)  0.84 us
    reshape x1, local copies, waits for them, and re-layouts, per_device(): moved.reshape(5, 16, 4, 32)[:, :rows, :3, :NZN].transpose(0, 1, 3, 2)  0.82 us

profile of v2, /device:TPU:0, one launch (start us, length us, event | category | flops | bytes accessed | tf_op | source)
XLA Modules:
  0.0 34.2 jit_solution(13661019090404391639)
XLA Ops:
  0.6 1.1 %maximum_bitcast_fusion = bf16[4,5,10,3,26]{4,3,2,1,0:T(4,128)(2,1)S(1)} fusion(bf16[1,5,10,26,3]{3,4,2,1,0:T(4,128)(2,1)} %bitcast.9, bf16[1,5,10,26,3]{3,4,2,1,0:T(4,128)(2,1)} %bitcast.10, bf16[1,5,10,26,3]{3,4,2,1,0:T(4,128)(2,1)} %bitcast.11, bf16[1,5,10,26,3]{3,4,2,1,0:T(4,128)(2,1)} %bitcast.12), kind=kLoop, calls=%fused_computation | loop fusion | flops 46800 | bytes 62400 | tf_op jit(solution)/shard_map/transpose | solution.py:552
  1.7 0.2 pad.4
  1.9 0.8 %reshape.12.prep = bf16[4,5,16,128]{3,2,1,0:T(8,128)(2,1)} reshape(bf16[4,5,16,4,32]{4,3,2,1,0:T(4,128)(2,1)S(1)} %pad.4) | data formatting | bytes 163840 | tf_op jit(solution)/shard_map/reshape | solution.py:554
  2.7 27.9 %shard_map.175 = (bf16[5,10,4992]{2,1,0:T(8,128)(2,1)}, bf16[5,16,128]{2,1,0:T(8,128)(2,1)}, f32[4,32]{1,0:T(4,128)}) custom-call(bf16[1,2,5]{2,1,0:T(2,128)(2,1)} %lam_ref.1, bf16[1,2,5]{2,1,0:T(2,128)(2,1)} %mu_ref.1, s32[1,2,5]{2,1,0:T(2,128)} %cell_ref.1, s32[1,64]{1,0:T(1,128)} %bitcast.13, bf16[5,10,4992]{2,1,0:T(8,128)(2,1)} %tan.1, ...), custom_call_target="tpu_custom_call" | custom-call | tf_op jit(solution)/shard_map/pallas_call | solution.py:565
  30.6 2.1 %shard_map.176 = (bf16[5,10,4992]{2,1,0:T(8,128)(2,1)}, f32[4,32]{1,0:T(4,128)}) custom-call(bf16[5,10,4992]{2,1,0:T(8,128)(2,1)} %get-tuple-element.9.tan, f32[4,32]{1,0:T(4,128)} %get-tuple-element.10.port), custom_call_target="tpu_custom_call" | custom-call | tf_op jit(solution)/shard_map/pallas_call | solution.py:612
  32.7 0.8 %reshape.13 = bf16[5,16,4,32]{3,2,1,0:T(4,128)(2,1)S(1)} reshape(bf16[5,16,128]{2,1,0:T(8,128)(2,1)} %get-tuple-element.8) | data formatting | bytes 40960 | tf_op jit(solution)/shard_map/reshape | solution.py:621
  33.6 0.6 %slice_bitcast_fusion = bf16[5,10,26,3]{2,3,1,0:T(4,128)(2,1)} fusion(bf16[5,16,4,32]{3,2,1,0:T(4,128)(2,1)S(1)} %reshape.13), kind=kLoop, calls=%fused_computation.1 | loop fusion | bytes 15600 | tf_op jit(solution)/shard_map/transpose | solution.py:621

commit v3 on v2

--- a/solution.py
+++ b/solution.py
@@ -118,8 +118,9 @@
 
 def kernel(
     nx, ny, nsrc_y,
-    lam_ref, mu_ref, cell_ref, dir_ref, tan, tanp, prep, mass, pid, k_hbm, e_hbm, p_hbm, q_hbm,
-    tan_out, disp_out, port_out,
+    lam_ref, mu_ref, cell_ref, dir_ref, tan_hbm, tanp_hbm, now, past, load, mode, mass, pid, k_hbm, e_hbm, p_hbm, q_hbm,
+    tan_hbm_out, disp_out, port_out,
+    tan, tanp, tan_out, out_sem, prep,
     kv, ev, pv, qv, const_sem,
     txf, tpf, exf, wf, oh, oht, uu, ms, ps, dsc, z, o, zf, cf, fs, fpb,
     s1x, s1y, s1d, r1x, r1y, r1d, s2x, s2y, s2d, s2p, r2x, r2y, r2d, r2p,
@@ -129,10 +130,15 @@
     gy = lax.axis_index("gy")
     consts = [
         pltpu.make_async_copy(a, b, const_sem.at[i])
-        for i, (a, b) in enumerate(((e_hbm, ev), (p_hbm, pv), (k_hbm, kv), (q_hbm, qv)))
+        for i, (a, b) in enumerate(
+            (
+                (e_hbm, ev), (p_hbm, pv), (k_hbm, kv), (q_hbm, qv),
+                (tan_hbm, tan), (tanp_hbm, tanp),
+            )
+        )
     ]
-    for copy in consts:
-        copy.start()
+    for i in (4, 5, 0, 1, 2, 3):
+        consts[i].start()
 
     x_lo, x_hi = gx > 0, gx < nx - 1
     y_lo, y_hi = gy > 0, gy < ny - 1
@@ -165,15 +171,24 @@
     lax.fori_loop(0, nx * nsrc_y, greet, 0)
     expected = expected + is_src.astype(jnp.int32) * (n_all - 1)
 
+    def lanes(source, index, x):
+        for c in range(3):
+            prep[index, x, 0:10, 32 * c:32 * c + NZN] = source[x, :, c, :].astype(F32)
+
+    prep[...] = jnp.zeros_like(prep)
+    for x in range(5):
+        lanes(now, 0, x)
+
+    consts[4].wait()
     s1y[...] = jnp.zeros_like(s1y)
     s1d[...] = jnp.zeros_like(s1d)
-    layer = jnp.concatenate([tan[0], prep[0, 0, 0:10, :]], axis=1)
+    layer = jnp.concatenate([tan[0], prep[0, 0, 0:10, :].astype(BF16)], axis=1)
     for to, at in X_PACK:
         s1x[to] = layer[at]
     for x in range(5):
         s1y[x:x + 1, 0:COLS] = tan[x, 0:1, :]
-        s1y[x:x + 1, COLS:] = prep[0, x, 0:1, :]
-    row = jnp.concatenate([tan[0, 0:1, :], prep[0, 0, 0:1, :]], axis=1)
+        s1y[x:x + 1, COLS:] = prep[0, x, 0:1, :].astype(BF16)
+    row = jnp.concatenate([tan[0, 0:1, :], prep[0, 0, 0:1, :].astype(BF16)], axis=1)
     for r in range(14):
         width = min(384, WIDE - r * 384)
         s1d[r:r + 1, 0:width] = row[:, r * 384:r * 384 + width]
@@ -237,7 +252,9 @@
         txf[x, 8:16, :] = jnp.zeros((8, WIDE), F32)
         tpf[x, 8:16, :] = jnp.zeros((8, COLS), F32)
         txf[x, 0:10, 0:COLS] = tan[x].astype(F32)
-        txf[x, :, COLS:] = prep[0, x].astype(F32)
+        txf[x, :, COLS:] = prep[0, x]
+        for index, source in ((1, past), (2, load), (3, mode)):
+            lanes(source, index, x)
         tpf[x, 0:10, :] = tanp[x].astype(F32)
         ms[...] = jnp.ones_like(ms)
         ps[...] = jnp.full(ps.shape, PORTS, jnp.int32)
@@ -249,7 +266,7 @@
         inv_hi, inv_lo = hi_lo(STEP_SQUARED / ms[...])
         exf[x, 0:16] = dot(inv_hi, rep).astype(BF16)
         exf[x, 16:32] = dot(inv_lo, rep).astype(BF16)
-        exf[x, 32:48] = prep[3, x]
+        exf[x, 32:48] = prep[3, x].astype(BF16)
         ids = ps[...]
         rows = pl.ds(pl.multiple_of(x * 16, 16), 16)
         for pair in range(13):
@@ -257,6 +274,7 @@
             oh[pair, rows, :] = jnp.where(port == lane % 64, 1.0, 0.0)
         return carry
 
+    consts[5].wait()
     lax.fori_loop(0, 5, prepare, 0)
 
     @pl.when(is_src)
@@ -457,16 +475,21 @@
         scale = exf[x, 0:16].astype(F32) + exf[x, 16:32].astype(F32)
         moved = (
             2.0 * txf[x, :, COLS:]
-            - prep[1, x].astype(F32)
-            + scale * (prep[2, x].astype(F32) - fs[x, :, COLS:])
+            - prep[1, x]
+            + scale * (prep[2, x] - fs[x, :, COLS:])
         )
         disp_out[x] = moved.astype(BF16)
         return carry
 
+    outs = [
+        pltpu.make_async_copy(tan_out.at[x], tan_hbm_out.at[x], out_sem.at[x]) for x in range(5)
+    ]
     for x in (1, 2, 3):
         arrived(second[3 + x])
         add_row(x, r2y.at[x], COLS)
     lax.fori_loop(1, 4, finish, 0)
+    for x in (1, 2, 3):
+        outs[x].start()
     arrived(second[0])
     arrived(second[1])
     arrived(second[3])
@@ -474,9 +497,11 @@
     add_row(0, r2y.at[0], COLS)
     add_row(0, r2d, WIDE)
     finish(0, 0)
+    outs[0].start()
     arrived(second[7])
     add_row(4, r2y.at[4], COLS)
     finish(4, 0)
+    outs[4].start()
 
     per_row = PORTS // ny
     slot = gx * nsrc_y + (gy - first_src)
@@ -523,6 +548,8 @@
         mine = jnp.where(gx == h, acc[0:per_row, h * per_col:(h + 1) * per_col], mine)
     port_out[...] = mine
 
+    for copy in outs:
+        copy.wait()
     for item in first + second:
         sent(item)
 
@@ -537,9 +564,11 @@
         lax.fori_loop(0, n_all, drain, 0)
 
 
-def settle(tan, port, tan_out, port_out):
+def settle(tan, port, point, tan_out, port_out, point_out):
     tan_out[...] = tan[...]
     port_out[...] = port[...]
+    for c in range(3):
+        point_out[0, :, c, :] = point[0, 0:10, 32 * c:32 * c + NZN]
 
 
 def per_device(
@@ -549,9 +578,7 @@
 ):
     rows = disp.shape[1]
     nsrc_y = -(-PORT_DEPTH // rows)
-    stacked = jnp.stack([disp, disp_prev, force, port_mode]).transpose(0, 1, 2, 4, 3)
-    stacked = jnp.pad(stacked, ((0, 0), (0, 0), (0, 16 - rows), (0, 1), (0, 32 - NZN)))
-    prep = stacked.reshape(4, 5, 16, 128)
+    primal = [a.transpose(0, 1, 3, 2) for a in (disp, disp_prev, force, port_mode)]
     expand, gather, scatter = layout_tables()
     tables = element_tables()
     nsrc = nx * nsrc_y
@@ -569,14 +596,19 @@
             jax.ShapeDtypeStruct((5, 16, 128), BF16),
             jax.ShapeDtypeStruct((PORTS // ny, NT // nx), F32),
         ),
-        in_specs=[vmem] * 9 + [hbm] * 4,
-        out_specs=(vmem, vmem, vmem),
+        in_specs=[vmem] * 4 + [hbm] * 2 + [vmem] * 6 + [hbm] * 4,
+        out_specs=(hbm, vmem, vmem),
         scratch_shapes=[
+            pltpu.VMEM(tangent.shape, BF16),
+            pltpu.VMEM(tangent.shape, BF16),
+            pltpu.VMEM(tangent.shape, BF16),
+            pltpu.SemaphoreType.DMA((5,)),
+            pltpu.VMEM((4, 5, 16, 128), F32),
             pltpu.VMEM(tables.shape, BF16),
             pltpu.VMEM(expand.shape, BF16),
             pltpu.VMEM(gather.shape, BF16),
             pltpu.VMEM(scatter.shape, BF16),
-            pltpu.SemaphoreType.DMA((4,)),
+            pltpu.SemaphoreType.DMA((6,)),
             pltpu.VMEM((6, 16, WIDE), F32),
             pltpu.VMEM((5, 16, COLS), F32),
             pltpu.VMEM((5, 48, 128), BF16),
@@ -606,19 +638,24 @@
             collective_id=0, has_side_effects=True, vmem_limit_bytes=56 * 1024 * 1024
         ),
     )(
-        lame_lambda, lame_mu, cell_block, direction_block[None], tangent, tangent_prev, prep, node_mass, port_id,
+        lame_lambda, lame_mu, cell_block, direction_block[None], tangent, tangent_prev, *primal, node_mass, port_id,
         jnp.asarray(tables), jnp.asarray(expand), jnp.asarray(gather), jnp.asarray(scatter),
     )
-    tangent_next, port_amp = pl.pallas_call(
+    layer = pl.BlockSpec((1,) + tangent.shape[1:], lambda x: (x, 0, 0))
+    whole = pl.BlockSpec(port_amp.shape, lambda x: (0, 0))
+    points = pl.BlockSpec((1,) + primal[0].shape[1:], lambda x: (x, 0, 0, 0))
+    tangent_next, port_amp, moved = pl.pallas_call(
         settle,
+        grid=(5,),
         out_shape=(
             jax.ShapeDtypeStruct(tangent_next.shape, BF16),
             jax.ShapeDtypeStruct(port_amp.shape, F32),
+            jax.ShapeDtypeStruct(primal[0].shape, BF16),
         ),
-        in_specs=[vmem, vmem],
-        out_specs=(vmem, vmem),
-    )(tangent_next, port_amp)
-    moved = moved.reshape(5, 16, 4, 32)[:, :rows, :3, :NZN].transpose(0, 1, 3, 2)
+        in_specs=[layer, whole, pl.BlockSpec((1, 16, 128), lambda x: (x, 0, 0))],
+        out_specs=(layer, whole, points),
+    )(tangent_next, port_amp, moved)
+    moved = moved.transpose(0, 1, 3, 2)
     return moved, tangent_next, port_amp
 
 

time: 34.5 us -> 31.9 us (0.925)
  local copies, waits for them, and re-layouts: 2.46 us -> 0 us
  other arithmetic: 1.08 us -> 0 us
  Pallas kernels: 30 us -> 31 us
    pallas_call x1, Pallas kernels: 2.09 us -> 3.76 us  [per_device(): pl.pallas_call(settle, grid=(5,), out_shape=(jax.ShapeDtypeStruct(tangent...]
    reshape x2 -> x0, local copies, waits for them, and re-layouts: 1.66 us -> none  [the longest x1 0.84 us: per_device(): prep = stacked.reshape(4, 5, 16, 128)]
    transpose x1 -> x0, other arithmetic: 1.08 us -> none  [per_device(): jnp.stack([disp, disp_prev, force, port_mode]).transpose(0, 1, 2, 4, 3)]
    pallas_call x1, Pallas kernels: 27.9 us -> 27.2 us  [per_device(): pl.pallas_call(functools.partial(kernel, nx, ny, nsrc_y), out_shape=(jax....]
    transpose x1 -> x0, local copies, waits for them, and re-layouts: 0.64 us -> none  [per_device(): moved.reshape(5, 16, 4, 32)[:, :rows, :3, :NZN].transpose(0, 1, 3, 2)]
where the time goes in v3:
time: 31.9 us; the launch traced here: 31.6 us
  Pallas kernels  31 us (97%)
  between operations  0.64 us (2%)
    pallas_call x1, Pallas kernels, per_device(): pl.pallas_call(functools.partial(kernel, nx, ny, nsrc_y), out_shape=(jax....  27.2 us
    pallas_call x1, Pallas kernels, per_device(): pl.pallas_call(settle, grid=(5,), out_shape=(jax.ShapeDtypeStruct(tangent...  3.76 us

profile of v3, /device:TPU:0, one launch (start us, length us, event | category | flops | bytes accessed | tf_op | source)
XLA Modules:
  0.0 31.6 jit_solution(9878846837325314769)
XLA Ops:
  0.6 27.2 %shard_map.175 = (bf16[5,10,4992]{2,1,0:T(8,128)(2,1)}, bf16[5,16,128]{2,1,0:T(8,128)(2,1)}, f32[4,32]{1,0:T(4,128)}) custom-call(bf16[1,2,5]{2,1,0:T(2,128)(2,1)} %lam_ref.1, bf16[1,2,5]{2,1,0:T(2,128)(2,1)} %mu_ref.1, s32[1,2,5]{2,1,0:T(2,128)} %cell_ref.1, s32[1,64]{1,0:T(1,128)} %bitcast.10, bf16[5,10,4992]{2,1,0:T(8,128)(2,1)} %tan_hbm.1, ...), custom_call_target="tpu_custom_call" | custom-call | tf_op jit(solution)/shard_map/pallas_call | solution.py:592
  27.9 3.8 %shard_map.176 = (bf16[5,10,4992]{2,1,0:T(8,128)(2,1)}, f32[4,32]{1,0:T(4,128)}, bf16[5,10,3,26]{3,2,1,0:T(4,128)(2,1)}) custom-call(bf16[5,10,4992]{2,1,0:T(8,128)(2,1)} %get-tuple-element.9.tan, f32[4,32]{1,0:T(4,128)} %get-tuple-element.10.port, bf16[5,16,128]{2,1,0:T(8,128)(2,1)} %get-tuple-element.11.point), custom_call_target="tpu_custom_call" | custom-call | tf_op jit(solution)/shard_map/pallas_call | solution.py:647

commit v4 on v3

--- a/solution.py
+++ b/solution.py
@@ -32,7 +32,6 @@
 BF16 = jnp.bfloat16
 COLS = 3 * NZN * NT
 WIDE = COLS + 128
-SPLITS = 2
 PAIRS = ((0, 1), (2, 3), (5, 6), (7, 8), (4, 9))
 
 
@@ -72,7 +71,7 @@
     both = both.reshape(2, 6, 108, 6, 108)
     both = np.pad(both, ((0, 0), (0, 0), (0, 4), (0, 0), (0, 4))).reshape(2, 6, 112, 672)
     both = both.transpose(1, 0, 2, 3).reshape(6, 224, 672)
-    return np.stack(split_bf16(both)[:SPLITS])
+    return np.concatenate(split_bf16(both), axis=1)
 
 
 def layout_tables():
@@ -176,23 +175,12 @@
             prep[index, x, 0:10, 32 * c:32 * c + NZN] = source[x, :, c, :].astype(F32)
 
     prep[...] = jnp.zeros_like(prep)
-    for x in range(5):
-        lanes(now, 0, x)
+    lanes(now, 0, 0)
 
     consts[4].wait()
-    s1y[...] = jnp.zeros_like(s1y)
-    s1d[...] = jnp.zeros_like(s1d)
     layer = jnp.concatenate([tan[0], prep[0, 0, 0:10, :].astype(BF16)], axis=1)
     for to, at in X_PACK:
         s1x[to] = layer[at]
-    for x in range(5):
-        s1y[x:x + 1, 0:COLS] = tan[x, 0:1, :]
-        s1y[x:x + 1, COLS:] = prep[0, x, 0:1, :].astype(BF16)
-    row = jnp.concatenate([tan[0, 0:1, :], prep[0, 0, 0:1, :].astype(BF16)], axis=1)
-    for r in range(14):
-        width = min(384, WIDE - r * 384)
-        s1d[r:r + 1, 0:width] = row[:, r * 384:r * 384 + width]
-
     pl.semaphore_wait(barrier, expected)
 
     def remote(index, src, dst, dx, dy):
@@ -239,8 +227,20 @@
         def _():
             copy.wait_send()
 
-    for item in first:
-        start(item)
+    start(first[0])
+    s1y[...] = jnp.zeros_like(s1y)
+    s1d[...] = jnp.zeros_like(s1d)
+    for x in range(5):
+        if x > 0:
+            lanes(now, 0, x)
+        s1y[x:x + 1, 0:COLS] = tan[x, 0:1, :]
+        s1y[x:x + 1, COLS:] = prep[0, x, 0:1, :].astype(BF16)
+    row = s1y[0:1, :]
+    for r in range(14):
+        width = min(384, WIDE - r * 384)
+        s1d[r:r + 1, 0:width] = row[:, r * 384:r * 384 + width]
+    start(first[1])
+    start(first[2])
 
     lane = lax.broadcasted_iota(jnp.int32, (1, 128), 1)
     low_half = lane < 64
@@ -346,7 +346,8 @@
 
     def apply(x):
         rhs = z[...].reshape(672, 768)
-        o[x] = sum(dot(kv[s, x], rhs) for s in range(SPLITS))
+        full = dot(kv[x], rhs)
+        o[x] = full[0:224] + full[224:448]
 
     def per_element(values):
         return [values[e // 5:e // 5 + 1, e % 5:e % 5 + 1] for e in range(10)]
@@ -478,7 +479,8 @@
             - prep[1, x]
             + scale * (prep[2, x] - fs[x, :, COLS:])
         )
-        disp_out[x] = moved.astype(BF16)
+        for c in range(3):
+            disp_out[x, :, c, :] = moved[0:10, 32 * c:32 * c + NZN].astype(BF16)
         return carry
 
     outs = [
@@ -564,11 +566,19 @@
         lax.fori_loop(0, n_all, drain, 0)
 
 
-def settle(tan, port, point, tan_out, port_out, point_out):
-    tan_out[...] = tan[...]
+def settle(tan, port, point, tan_out, port_out, point_out, held, sem_in, sem_out):
+    layers = range(held.shape[0])
+    into = [pltpu.make_async_copy(tan.at[x], held.at[x], sem_in.at[x]) for x in layers]
+    out = [pltpu.make_async_copy(held.at[x], tan_out.at[x], sem_out.at[x]) for x in layers]
+    for copy in into:
+        copy.start()
     port_out[...] = port[...]
-    for c in range(3):
-        point_out[0, :, c, :] = point[0, 0:10, 32 * c:32 * c + NZN]
+    point_out[...] = point[...]
+    for x in layers:
+        into[x].wait()
+        out[x].start()
+    for copy in out:
+        copy.wait()
 
 
 def per_device(
@@ -593,7 +603,7 @@
         functools.partial(kernel, nx, ny, nsrc_y),
         out_shape=(
             jax.ShapeDtypeStruct(tangent.shape, BF16),
-            jax.ShapeDtypeStruct((5, 16, 128), BF16),
+            jax.ShapeDtypeStruct(primal[0].shape, BF16),
             jax.ShapeDtypeStruct((PORTS // ny, NT // nx), F32),
         ),
         in_specs=[vmem] * 4 + [hbm] * 2 + [vmem] * 6 + [hbm] * 4,
@@ -641,19 +651,20 @@
         lame_lambda, lame_mu, cell_block, direction_block[None], tangent, tangent_prev, *primal, node_mass, port_id,
         jnp.asarray(tables), jnp.asarray(expand), jnp.asarray(gather), jnp.asarray(scatter),
     )
-    layer = pl.BlockSpec((1,) + tangent.shape[1:], lambda x: (x, 0, 0))
-    whole = pl.BlockSpec(port_amp.shape, lambda x: (0, 0))
-    points = pl.BlockSpec((1,) + primal[0].shape[1:], lambda x: (x, 0, 0, 0))
     tangent_next, port_amp, moved = pl.pallas_call(
         settle,
-        grid=(5,),
         out_shape=(
             jax.ShapeDtypeStruct(tangent_next.shape, BF16),
             jax.ShapeDtypeStruct(port_amp.shape, F32),
-            jax.ShapeDtypeStruct(primal[0].shape, BF16),
+            jax.ShapeDtypeStruct(moved.shape, BF16),
         ),
-        in_specs=[layer, whole, pl.BlockSpec((1, 16, 128), lambda x: (x, 0, 0))],
-        out_specs=(layer, whole, points),
+        in_specs=[hbm, vmem, vmem],
+        out_specs=(hbm, vmem, vmem),
+        scratch_shapes=[
+            pltpu.VMEM(tangent.shape, BF16),
+            pltpu.SemaphoreType.DMA((5,)),
+            pltpu.SemaphoreType.DMA((5,)),
+        ],
     )(tangent_next, port_amp, moved)
     moved = moved.transpose(0, 1, 3, 2)
     return moved, tangent_next, port_amp

time: 31.9 us -> 31.7 us (level)
    pallas_call x1, Pallas kernels: 3.76 us -> 3.41 us  [per_device(): pl.pallas_call(settle, out_shape=(jax.ShapeDtypeStruct(tangent_next.shape...]
where the time goes in v4:
time: 31.7 us; the launch traced here: 31.4 us
  Pallas kernels  30.8 us (97%)
  between operations  0.64 us (2%)
    pallas_call x1, Pallas kernels, per_device(): pl.pallas_call(functools.partial(kernel, nx, ny, nsrc_y), out_shape=(jax....  27.4 us
    pallas_call x1, Pallas kernels, per_device(): pl.pallas_call(settle, out_shape=(jax.ShapeDtypeStruct(tangent_next.shape...  3.41 us

profile of v4, /device:TPU:0, one launch (start us, length us, event | category | flops | bytes accessed | tf_op | source)
XLA Modules:
  0.0 31.4 jit_solution(10328605879352020784)
XLA Ops:
  0.6 27.4 %shard_map.175 = (bf16[5,10,4992]{2,1,0:T(8,128)(2,1)}, bf16[5,10,3,26]{3,2,1,0:T(4,128)(2,1)}, f32[4,32]{1,0:T(4,128)}) custom-call(bf16[1,2,5]{2,1,0:T(2,128)(2,1)} %lam_ref.1, bf16[1,2,5]{2,1,0:T(2,128)(2,1)} %mu_ref.1, s32[1,2,5]{2,1,0:T(2,128)} %cell_ref.1, s32[1,64]{1,0:T(1,128)} %bitcast.10, bf16[5,10,4992]{2,1,0:T(8,128)(2,1)} %tan_hbm.1, ...), custom_call_target="tpu_custom_call" | custom-call | tf_op jit(solution)/shard_map/pallas_call | solution.py:602
  28.0 3.4 %shard_map.176 = (bf16[5,10,4992]{2,1,0:T(8,128)(2,1)}, f32[4,32]{1,0:T(4,128)}, bf16[5,10,3,26]{3,2,1,0:T(4,128)(2,1)}) custom-call(bf16[5,10,4992]{2,1,0:T(8,128)(2,1)} %get-tuple-element.9.tan, f32[4,32]{1,0:T(4,128)} %get-tuple-element.10.port, bf16[5,10,3,26]{3,2,1,0:T(4,128)(2,1)} %get-tuple-element.11.point), custom_call_target="tpu_custom_call" | custom-call | tf_op jit(solution)/shard_map/pallas_call | solution.py:654

commit v5 on v4

--- a/solution.py
+++ b/solution.py
@@ -566,19 +566,10 @@
         lax.fori_loop(0, n_all, drain, 0)
 
 
-def settle(tan, port, point, tan_out, port_out, point_out, held, sem_in, sem_out):
-    layers = range(held.shape[0])
-    into = [pltpu.make_async_copy(tan.at[x], held.at[x], sem_in.at[x]) for x in layers]
-    out = [pltpu.make_async_copy(held.at[x], tan_out.at[x], sem_out.at[x]) for x in layers]
-    for copy in into:
-        copy.start()
+def settle(tan, port, point, tan_out, port_out, point_out):
+    tan_out[...] = tan[...]
     port_out[...] = port[...]
     point_out[...] = point[...]
-    for x in layers:
-        into[x].wait()
-        out[x].start()
-    for copy in out:
-        copy.wait()
 
 
 def per_device(
@@ -658,13 +649,8 @@
             jax.ShapeDtypeStruct(port_amp.shape, F32),
             jax.ShapeDtypeStruct(moved.shape, BF16),
         ),
-        in_specs=[hbm, vmem, vmem],
-        out_specs=(hbm, vmem, vmem),
-        scratch_shapes=[
-            pltpu.VMEM(tangent.shape, BF16),
-            pltpu.SemaphoreType.DMA((5,)),
-            pltpu.SemaphoreType.DMA((5,)),
-        ],
+        in_specs=[vmem] * 3,
+        out_specs=(vmem, vmem, vmem),
     )(tangent_next, port_amp, moved)
     moved = moved.transpose(0, 1, 3, 2)
     return moved, tangent_next, port_amp

time: 31.7 us -> 30.3 us (0.956)
  Pallas kernels: 30.8 us -> 29.5 us
    pallas_call x1, Pallas kernels: 3.41 us -> 2.12 us  [per_device(): pl.pallas_call(settle, out_shape=(jax.ShapeDtypeStruct(tangent_next.shape...]
where the time goes in v5:
time: 30.3 us; the launch traced here: 30.1 us
  Pallas kernels  29.5 us (97%)
  between operations  0.64 us (2%)
    pallas_call x1, Pallas kernels, per_device(): pl.pallas_call(functools.partial(kernel, nx, ny, nsrc_y), out_shape=(jax....  27.4 us
    pallas_call x1, Pallas kernels, per_device(): pl.pallas_call(settle, out_shape=(jax.ShapeDtypeStruct(tangent_next.shape...  2.12 us

profile of v5, /device:TPU:0, one launch (start us, length us, event | category | flops | bytes accessed | tf_op | source)
XLA Modules:
  0.0 30.1 jit_solution(7930707462352396135)
XLA Ops:
  0.6 27.4 %shard_map.175 = (bf16[5,10,4992]{2,1,0:T(8,128)(2,1)}, bf16[5,10,3,26]{3,2,1,0:T(4,128)(2,1)}, f32[4,32]{1,0:T(4,128)}) custom-call(bf16[1,2,5]{2,1,0:T(2,128)(2,1)} %lam_ref.1, bf16[1,2,5]{2,1,0:T(2,128)(2,1)} %mu_ref.1, s32[1,2,5]{2,1,0:T(2,128)} %cell_ref.1, s32[1,64]{1,0:T(1,128)} %bitcast.10, bf16[5,10,4992]{2,1,0:T(8,128)(2,1)} %tan_hbm.1, ...), custom_call_target="tpu_custom_call" | custom-call | tf_op jit(solution)/shard_map/pallas_call | solution.py:593
  28.0 2.1 %shard_map.176 = (bf16[5,10,4992]{2,1,0:T(8,128)(2,1)}, f32[4,32]{1,0:T(4,128)}, bf16[5,10,3,26]{3,2,1,0:T(4,128)(2,1)}) custom-call(bf16[5,10,4992]{2,1,0:T(8,128)(2,1)} %get-tuple-element.9.tan, f32[4,32]{1,0:T(4,128)} %get-tuple-element.10.port, bf16[5,10,3,26]{3,2,1,0:T(4,128)(2,1)} %get-tuple-element.11.point), custom_call_target="tpu_custom_call" | custom-call | tf_op jit(solution)/shard_map/pallas_call | solution.py:645
